TPU v7x, 128 devices: a whole 4x4x4 slice. The times are simulated.
128 devices in a mesh: depth: 8 (over z, y_lo), height: 16 (over x, y_hi, core).
Axes of the slice: x: 4, y: 4 (y_hi: 2, y_lo: 2; y = y_hi * 2 + y_lo), z: 4, core: 2. Of those that a mesh axis runs over, the one named last changes fastest.
Arguments:
- volume: bfloat16 [32, 32, 128, 128], P(None, 'depth', 'height'), may hold values from -6 to 6
- filters_three: bfloat16 [27, 64, 32], replicated, may hold values from -0.21875 to 0.21875
- filters_four: bfloat16 [27, 128, 64], P(None, 'height'), may hold values from -0.15625 to 0.15625
- cotangent: bfloat16 [128, 16, 64, 64], P(None, 'depth', 'height'), may hold values from -6 to 6
Outputs:
- grad_volume: bfloat16 [32, 32, 128, 128], P(None, 'depth', 'height')
- grad_three: float32 [27, 64, 32], replicated
- grad_four: float32 [27, 128, 64], P(None, 'height')
All inputs are finite; a program needn't handle non-finite values.
Results may differ from a plain program's by a relative error of at most 0.023.
Values may be sent and summed in bfloat16 or wider, within the bound.
A program may use at most 256 MiB of HBM per device.

v0:
```python
import math
import jax
import jax.numpy as jnp
from jax import lax
from jax.sharding import PartitionSpec as P

TANH_SCALE = 0.7978845608028654
CUBIC_TERM = 0.044715


def extended_2(x, sides, width):
    for axis, dim in sides:
        size, length = (lax.axis_size(axis), x.shape[dim])
        up = [(i, (i + 1) % size) for i in range(size - 1)]
        down = [(j, i) for i, j in up]
        last = lax.slice_in_dim(x, length - width, length, axis=dim)
        first = lax.slice_in_dim(x, 0, width, axis=dim)
        before = lax.ppermute(last, axis, up)
        after = lax.ppermute(first, axis, down)
        x = jnp.concatenate([before, x, after], axis=dim)
    return x


def gelu_value(values_in):
    inner = jnp.tanh(TANH_SCALE * (values_in + CUBIC_TERM * values_in * values_in * values_in))
    return 0.5 * values_in * (1.0 + inner)


def gelu_slope(values_in):
    inner = jnp.tanh(TANH_SCALE * (values_in + CUBIC_TERM * values_in * values_in * values_in))
    return 0.5 * (1.0 + inner) + 0.5 * values_in * (1.0 - inner * inner) * TANH_SCALE * (
        1.0 + 3.0 * CUBIC_TERM * values_in * values_in
    )


def pad_width(values_in):
    return jnp.pad(values_in, ((0, 0), (0, 0), (0, 0), (1, 1)))


def forward_taps(padded, weights, depth_cells, height_cells, width_cells):
    running = jnp.zeros((weights.shape[1], depth_cells, height_cells, width_cells), jnp.float32)
    for first in range(3):
        for second in range(3):
            for third in range(3):
                window_piece = padded[
                    :,
                    first : first + depth_cells,
                    second : second + height_cells,
                    third : third + width_cells,
                ]
                running = running + jnp.einsum(
                    "oi,idhw->odhw",
                    weights[9 * first + 3 * second + third],
                    window_piece,
                    preferred_element_type=jnp.float32,
                )
    return running


def transpose_taps(padded, weights, depth_cells, height_cells, width_cells):
    running = jnp.zeros((weights.shape[2], depth_cells, height_cells, width_cells), jnp.float32)
    for first in range(3):
        for second in range(3):
            for third in range(3):
                window_piece = padded[
                    :,
                    2 - first : 2 - first + depth_cells,
                    2 - second : 2 - second + height_cells,
                    2 - third : 2 - third + width_cells,
                ]
                running = running + jnp.einsum(
                    "oi,odhw->idhw",
                    weights[9 * first + 3 * second + third],
                    window_piece,
                    preferred_element_type=jnp.float32,
                )
    return running


def weight_taps(delta, padded, depth_cells, height_cells, width_cells):
    collected = []
    for first in range(3):
        for second in range(3):
            for third in range(3):
                window_piece = padded[
                    :,
                    first : first + depth_cells,
                    second : second + height_cells,
                    third : third + width_cells,
                ]
                collected.append(
                    jnp.einsum(
                        "odhw,idhw->oi", delta, window_piece, preferred_element_type=jnp.float32
                    )
                )
    return jnp.stack(collected, axis=0)


def shards(volume, filters_three, filters_four, cotangent):
    channels_in, depth_cells, height_cells, width_cells = volume.shape
    depth_count = lax.axis_size("depth")
    height_count = lax.axis_size("height")
    scale_three = 1.0 / math.sqrt(
        depth_cells * depth_count * height_cells * height_count * width_cells
    )
    scale_four = 1.0 / math.sqrt(
        depth_cells * depth_count // 2 * (height_cells * height_count // 2) * (width_cells // 2)
    )
    half_depth = depth_cells // 2
    half_height = height_cells // 2
    half_width = width_cells // 2
    extended = extended_2(volume, (("depth", 1), ("height", 2)), 1)
    padded = pad_width(extended)
    act_three = forward_taps(padded, filters_three, depth_cells, height_cells, width_cells)
    channels_mid = act_three.shape[0]
    hidden = gelu_value(act_three).reshape(
        channels_mid, half_depth, 2, half_height, 2, half_width, 2
    )
    pooled = (jnp.sum(hidden, axis=(2, 4, 6)) * 0.125).astype(jnp.bfloat16)
    full_bank = lax.all_gather(filters_four, "height", axis=1, tiled=True)
    rimmed = extended_2(pooled, (("depth", 1), ("height", 2)), 1)
    pooled_pad = pad_width(rimmed)
    act_four = forward_taps(pooled_pad, full_bank, half_depth, half_height, half_width)
    delta_four = (cotangent.astype(jnp.float32) * gelu_slope(act_four)).astype(jnp.bfloat16)
    partial_four = weight_taps(delta_four, pooled_pad, half_depth, half_height, half_width)
    depth_summed = lax.psum(partial_four.astype(jnp.bfloat16), "depth")
    grad_four = (
        lax.psum_scatter(depth_summed, "height", scatter_dimension=1, tiled=True).astype(
            jnp.float32
        )
        * scale_four
    )
    delta_rim = extended_2(delta_four, (("depth", 1), ("height", 2)), 1)
    back_pooled = transpose_taps(
        pad_width(delta_rim), full_bank, half_depth, half_height, half_width
    )
    spread = (
        jnp.repeat(jnp.repeat(jnp.repeat(back_pooled, 2, axis=1), 2, axis=2), 2, axis=3) * 0.125
    )
    delta_three = (spread * gelu_slope(act_three)).astype(jnp.bfloat16)
    partial_three = weight_taps(delta_three, padded, depth_cells, height_cells, width_cells)
    grad_three = lax.psum(partial_three, ("depth", "height")) * scale_three
    delta_extended = extended_2(delta_three, (("depth", 1), ("height", 2)), 1)
    grad_volume = transpose_taps(
        pad_width(delta_extended), filters_three, depth_cells, height_cells, width_cells
    ).astype(jnp.bfloat16)
    return (grad_volume, grad_three, grad_four)


def solution(mesh):
    in_specs = (
        P(None, "depth", "height", None),
        P(),
        P(None, "height", None),
        P(None, "depth", "height", None),
    )
    out_specs = (P(None, "depth", "height", None), P(), P(None, "height", None))
    return jax.shard_map(shards, mesh=mesh, in_specs=in_specs, out_specs=out_specs, check_vma=False)
```

profile of v0, /device:TPU:6, one launch (start us, length us, event | category | flops | bytes accessed | tf_op | source)
XLA Modules:
  0.0 348.1 jit_solution(2866375884435285282)
XLA Ops:
  8.1 0.9 fusion.559
  9.0 3.5 %collective-permute-start = (bf16[32,1,8,128]{3,0,2,1:T(8,128)(2,1)S(1)}, bf16[32,1,8,128]{3,0,2,1:T(8,128)(2,1)S(1)}, u32[]{:S(2)}, u32[]{:S(2)}) collective-permute-start(bf16[32,1,8,128]{3,0,2,1:T(8,128)(2,1)S(1)} %copy.321), channel_id=1, source_target_pairs={{0,16},{16,32},{32,48},{48,64},{64,80},{80,96},{96,112},{1,17},{17... | collective-permute-start | bytes 196616 | tf_op jit(solution)/shard_map/ppermute | solution.py:18
  12.5 1.3 collective-permute-start.1
  13.8 0.6 collective-permute-done
  14.4 1.2 constant_dynamic-update-slice_fusion.6
  15.6 3.1 collective-permute-done.1
  18.8 1.9 collective-permute-start.2
  20.7 6.0 %collective-permute-start.3 = (bf16[32,6,1,128]{3,0,2,1:T(8,128)(2,1)S(1)}, bf16[32,6,1,128]{3,0,2,1:T(8,128)(2,1)S(1)}, u32[]{:S(2)}, u32[]{:S(2)}) collective-permute-start(bf16[32,6,1,128]{3,0,2,1:T(8,128)(2,1)S(1)} %get-tuple-element.19), channel_id=1, source_target_pairs={{1,0},{2,1},{3,2},{4,3},{5,4},{6,5},{7,6},{8,7},{9,8},{10,9},{11,1... | collective-permute-start | bytes 147464 | tf_op jit(solution)/shard_map/ppermute | solution.py:19
  27.1 1.4 collective-permute-done.3
  28.5 0.5 fusion.212
  29.3 0.4 fusion.320
  30.0 0.4 fusion.314
  30.7 0.4 fusion.308
  31.1 0.4 convolution_bitcast_fusion.10
  32.2 0.4 convolution_bitcast_fusion.8
  32.9 0.4 convolution_bitcast_fusion.4
  33.7 0.4 convolution_bitcast_fusion.6
  34.7 0.4 convolution_add_fusion.4
  36.9 0.4 fusion.22
  37.3 0.7 fusion.27
  38.3 2.0 add_multiply_fusion
  40.4 1.8 copy.91
  42.2 2.4 reduce_sum.9
  44.6 1.0 multiply_convert_fusion
  45.6 4.6 %collective-permute-start.4 = (bf16[64,1,4,64]{0,3,2,1:T(8,128)(2,1)S(1)}, bf16[64,1,4,64]{0,3,2,1:T(8,128)(2,1)S(1)}, u32[]{:S(2)}, u32[]{:S(2)}) collective-permute-start(bf16[64,1,4,64]{0,3,2,1:T(8,128)(2,1)S(1)} %get-tuple-element.33), channel_id=1, source_target_pairs={{0,16},{16,32},{32,48},{48,64},{64,80},{80,96},{96,112},{1,17},{17... | collective-permute-start | bytes 98312 | tf_op jit(solution)/shard_map/ppermute | solution.py:18
  50.2 1.3 collective-permute-start.5
  51.5 23.7 %all_gather.3 = bf16[27,128,64]{2,1,0:T(8,128)(2,1)S(1)} all-gather(bf16[27,8,64]{2,1,0:T(8,128)(2,1)S(1)} %copy-done.14), channel_id=1, replica_groups=mesh['depth'=8,'height'=16] {'height'}, dimensions={1}, use_global_device_ids=true | all-gather | bytes 470016 | tf_op jit(solution)/shard_map/all_gather | solution.py:120
  75.2 2.3 collective-permute-start.6
  77.5 5.7 %collective-permute-start.7 = (bf16[64,4,1,64]{0,3,2,1:T(8,128)(2,1)S(1)}, bf16[64,4,1,64]{0,3,2,1:T(8,128)(2,1)S(1)}, u32[]{:S(2)}, u32[]{:S(2)}) collective-permute-start(bf16[64,4,1,64]{0,3,2,1:T(8,128)(2,1)S(1)} %get-tuple-element.25), channel_id=1, source_target_pairs={{1,0},{2,1},{3,2},{4,3},{5,4},{6,5},{7,6},{8,7},{9,8},{10,9},{11,1... | collective-permute-start | bytes 98312 | tf_op jit(solution)/shard_map/ppermute | solution.py:19
  83.4 1.7 collective-permute-done.7
  90.5 0.4 fusion.283
  96.6 4.0 %collective-permute-start.8 = (bf16[128,1,4,64]{0,3,2,1:T(8,128)(2,1)S(1)}, bf16[128,1,4,64]{0,3,2,1:T(8,128)(2,1)S(1)}, u32[]{:S(2)}, u32[]{:S(2)}) collective-permute-start(bf16[128,1,4,64]{0,3,2,1:T(8,128)(2,1)S(1)} %get-tuple-element.31), channel_id=1, source_target_pairs={{0,16},{16,32},{32,48},{48,64},{64,80},{80,96},{96,112},{1,17},{17... | collective-permute-start | bytes 196616 | tf_op jit(solution)/shard_map/ppermute | solution.py:18
  100.5 1.3 collective-permute-start.9
  102.0 0.9 collective-permute-done.8
  102.9 4.1 %collective-permute-done.9 = bf16[128,1,4,64]{0,3,2,1:T(8,128)(2,1)S(1)} collective-permute-done((bf16[128,1,4,64]{0,3,2,1:T(8,128)(2,1)S(1)}, bf16[128,1,4,64]{0,3,2,1:T(8,128)(2,1)S(1)}, u32[]{:S(2)}, u32[]{:S(2)}) %collective-permute-start.9) | collective-permute-done | bytes 65568 | tf_op jit(solution)/shard_map/ppermute | solution.py:19
  107.1 4.9 %collective-permute-start.11 = (bf16[128,4,1,64]{0,3,2,1:T(8,128)(2,1)S(1)}, bf16[128,4,1,64]{0,3,2,1:T(8,128)(2,1)S(1)}, u32[]{:S(2)}, u32[]{:S(2)}) collective-permute-start(bf16[128,4,1,64]{0,3,2,1:T(8,128)(2,1)S(1)} %get-tuple-element.23), channel_id=1, source_target_pairs={{1,0},{2,1},{3,2},{4,3},{5,4},{6,5},{7,6},{8,7},{9,8},{10,9},{11,1... | collective-permute-start | bytes 196616 | tf_op jit(solution)/shard_map/ppermute | solution.py:19
  112.0 1.9 collective-permute-start.10
  114.2 5.8 %collective-permute-done.10 = bf16[128,4,1,64]{0,3,2,1:T(8,128)(2,1)S(1)} collective-permute-done((bf16[128,4,1,64]{0,3,2,1:T(8,128)(2,1)S(1)}, bf16[128,4,1,64]{0,3,2,1:T(8,128)(2,1)S(1)}, u32[]{:S(2)}, u32[]{:S(2)}) %collective-permute-start.10) | collective-permute-done | bytes 65568 | tf_op jit(solution)/shard_map/ppermute | solution.py:18
  125.1 0.4 broadcast_in_dim.10
  125.5 1.5 broadcast_in_dim.11
  127.0 2.2 copy.120
  129.2 1.9 fusion.210
  139.0 0.7 copy-done.12
  139.8 0.8 fusion.124
  140.7 3.3 copy.149
  144.3 1.3 collective-permute-start.13
  145.6 4.6 %collective-permute-start.12 = (bf16[64,1,8,128]{3,0,2,1:T(8,128)(2,1)S(1)}, bf16[64,1,8,128]{3,0,2,1:T(8,128)(2,1)S(1)}, u32[]{:S(2)}, u32[]{:S(2)}) collective-permute-start(bf16[64,1,8,128]{3,0,2,1:T(8,128)(2,1)S(1)} %get-tuple-element.16), channel_id=1, source_target_pairs={{0,16},{16,32},{32,48},{48,64},{64,80},{80,96},{96,112},{1,17},{17... | collective-permute-start | bytes 393224 | tf_op jit(solution)/shard_map/ppermute | solution.py:18
  150.1 134.6 %all-reduce.6.cloned.1.call-done = f32[27,64,32]{1,2,0:T(8,128)} async-done(((f32[27,64,32]{1,2,0:T(8,128)}), f32[27,64,32]{1,2,0:T(8,128)}) %all-reduce.6.cloned.1.call-update) | async-done | bytes 221200 | tf_op jit(solution)/shard_map/psum | solution.py:142
  284.7 1.8 broadcast_multiply_fusion
  286.6 1.9 collective-permute-start.14
  288.5 6.3 %collective-permute-start.15 = (bf16[64,6,1,128]{3,0,2,1:T(8,128)(2,1)S(1)}, bf16[64,6,1,128]{3,0,2,1:T(8,128)(2,1)S(1)}, u32[]{:S(2)}, u32[]{:S(2)}) collective-permute-start(bf16[64,6,1,128]{3,0,2,1:T(8,128)(2,1)S(1)} %get-tuple-element.15), channel_id=1, source_target_pairs={{1,0},{2,1},{3,2},{4,3},{5,4},{6,5},{7,6},{8,7},{9,8},{10,9},{11,1... | collective-permute-start | bytes 294920 | tf_op jit(solution)/shard_map/ppermute | solution.py:19
  295.2 1.5 collective-permute-done.15
  297.3 1.8 select_maximum_fusion
  299.7 0.4 fusion.236
  300.3 0.4 fusion.242
  300.9 0.4 fusion.248
  301.9 0.4 fusion.227
  302.9 0.4 convolution_bitcast_fusion.15
  303.5 0.4 convolution_bitcast_fusion.18
  304.4 0.7 fusion.52
  305.3 0.4 fusion.53
  305.8 0.8 copy.150
  306.6 33.3 %psum.16 = bf16[27,8,64]{2,0,1:T(8,128)(2,1)S(1)} all-reduce(bf16[27,8,64]{2,0,1:T(8,128)(2,1)} %reduce-scatter.2.cloned.1.call-done), channel_id=1, replica_groups=mesh['depth'=8,'height'=16] {'depth'}, use_global_device_ids=true, to_apply=%region_2.3 | all-reduce | flops 13824 | bytes 55296 | tf_op jit(solution)/shard_map/psum | solution.py:126
  339.9 0.7 copy.151
  (203 shorter events, 34.6 us)
Async XLA Ops:
  8.0 18.7 %copy-start = (bf16[32,4,8,128]{3,2,1,0:T(8,128)(2,1)S(1)}, bf16[32,4,8,128]{3,2,1,0:T(8,128)(2,1)}, u32[]{:S(2)}) copy-start(bf16[32,4,8,128]{3,2,1,0:T(8,128)(2,1)} %param.4) | copy-start | bytes 786436
  8.0 18.7 %copy-start.6 = (bf16[27,64,32]{1,2,0:T(8,128)(2,1)S(1)}, bf16[27,64,32]{1,2,0:T(8,128)(2,1)}, u32[]{:S(2)}) copy-start(bf16[27,64,32]{1,2,0:T(8,128)(2,1)} %param.5) | copy-start | bytes 331780
  8.0 276.7 %all-reduce.6.cloned.1.call-start = ((), (), s32[]{:S(2)}) async-start(), calls=%async_computation.1 | async-start | bytes 884736 | tf_op jit(solution)/shard_map/psum | solution.py:142
  9.0 5.4 %collective-permute-start = (bf16[32,1,8,128]{3,0,2,1:T(8,128)(2,1)S(1)}, bf16[32,1,8,128]{3,0,2,1:T(8,128)(2,1)S(1)}, u32[]{:S(2)}, u32[]{:S(2)}) collective-permute-start(bf16[32,1,8,128]{3,0,2,1:T(8,128)(2,1)S(1)} %copy.321), channel_id=1, source_target_pairs={{0,16},{16,32},{32,48},{48,64},{64,80},{80,96},{96,112},{1,17},{17... | collective-permute-start | bytes 196616 | tf_op jit(solution)/shard_map/ppermute | solution.py:18
  12.5 6.2 %collective-permute-start.1 = (bf16[32,1,8,128]{3,0,2,1:T(8,128)(2,1)S(1)}, bf16[32,1,8,128]{3,0,2,1:T(8,128)(2,1)S(1)}, u32[]{:S(2)}, u32[]{:S(2)}) collective-permute-start(bf16[32,1,8,128]{3,0,2,1:T(8,128)(2,1)S(1)} %copy.322), channel_id=1, source_target_pairs={{16,0},{32,16},{48,32},{64,48},{80,64},{96,80},{112,96},{17,1},{33... | collective-permute-start | bytes 196616 | tf_op jit(solution)/shard_map/ppermute | solution.py:19
  15.6 19.9 %copy-start.4 = (bf16[32,5,8,128]{3,0,2,1:T(8,128)(2,1)}, bf16[32,5,8,128]{3,0,2,1:T(8,128)(2,1)S(1)}, u32[]{:S(2)}) copy-start(bf16[32,5,8,128]{3,0,2,1:T(8,128)(2,1)S(1)} %get-tuple-element.28) | copy-start | bytes 983044
  18.7 19.6 %copy-start.2 = (bf16[32,5,8,128]{3,0,2,1:T(8,128)(2,1)}, bf16[32,5,8,128]{3,0,2,1:T(8,128)(2,1)S(1)}, u32[]{:S(2)}) copy-start(bf16[32,5,8,128]{3,0,2,1:T(8,128)(2,1)S(1)} %get-tuple-element.35) | copy-start | bytes 983044
  18.8 8.3 %collective-permute-start.2 = (bf16[32,6,1,128]{3,0,2,1:T(8,128)(2,1)S(1)}, bf16[32,6,1,128]{3,0,2,1:T(8,128)(2,1)S(1)}, u32[]{:S(2)}, u32[]{:S(2)}) collective-permute-start(bf16[32,6,1,128]{3,0,2,1:T(8,128)(2,1)S(1)} %get-tuple-element.18), channel_id=1, source_target_pairs={{0,1},{1,2},{2,3},{3,4},{4,5},{5,6},{6,7},{7,8},{8,9},{9,10},{10,1... | collective-permute-start | bytes 147464 | tf_op jit(solution)/shard_map/ppermute | solution.py:18
  20.7 7.8 %collective-permute-start.3 = (bf16[32,6,1,128]{3,0,2,1:T(8,128)(2,1)S(1)}, bf16[32,6,1,128]{3,0,2,1:T(8,128)(2,1)S(1)}, u32[]{:S(2)}, u32[]{:S(2)}) collective-permute-start(bf16[32,6,1,128]{3,0,2,1:T(8,128)(2,1)S(1)} %get-tuple-element.19), channel_id=1, source_target_pairs={{1,0},{2,1},{3,2},{4,3},{5,4},{6,5},{7,6},{8,7},{9,8},{10,9},{11,1... | collective-permute-start | bytes 147464 | tf_op jit(solution)/shard_map/ppermute | solution.py:19
  27.1 9.8 %copy-start.10 = (bf16[32,6,1,128]{3,0,2,1:T(8,128)(2,1)}, bf16[32,6,1,128]{3,0,2,1:T(8,128)(2,1)S(1)}, u32[]{:S(2)}) copy-start(bf16[32,6,1,128]{3,0,2,1:T(8,128)(2,1)S(1)} %collective-permute-done.2) | copy-start | bytes 147460
  28.5 9.5 %copy-start.8 = (bf16[32,6,1,128]{3,0,2,1:T(8,128)(2,1)}, bf16[32,6,1,128]{3,0,2,1:T(8,128)(2,1)S(1)}, u32[]{:S(2)}) copy-start(bf16[32,6,1,128]{3,0,2,1:T(8,128)(2,1)S(1)} %collective-permute-done.3) | copy-start | bytes 147460
  42.2 9.3 %copy-start.14 = (bf16[27,8,64]{2,1,0:T(8,128)(2,1)S(1)}, bf16[27,8,64]{2,1,0:T(8,128)(2,1)}, u32[]{:S(2)}) copy-start(bf16[27,8,64]{2,1,0:T(8,128)(2,1)} %param.6) | copy-start | bytes 82948
  45.6 29.6 %collective-permute-start.4 = (bf16[64,1,4,64]{0,3,2,1:T(8,128)(2,1)S(1)}, bf16[64,1,4,64]{0,3,2,1:T(8,128)(2,1)S(1)}, u32[]{:S(2)}, u32[]{:S(2)}) collective-permute-start(bf16[64,1,4,64]{0,3,2,1:T(8,128)(2,1)S(1)} %get-tuple-element.33), channel_id=1, source_target_pairs={{0,16},{16,32},{32,48},{48,64},{64,80},{80,96},{96,112},{1,17},{17... | collective-permute-start | bytes 98312 | tf_op jit(solution)/shard_map/ppermute | solution.py:18
  50.2 25.0 %collective-permute-start.5 = (bf16[64,1,4,64]{0,3,2,1:T(8,128)(2,1)S(1)}, bf16[64,1,4,64]{0,3,2,1:T(8,128)(2,1)S(1)}, u32[]{:S(2)}, u32[]{:S(2)}) collective-permute-start(bf16[64,1,4,64]{0,3,2,1:T(8,128)(2,1)S(1)} %get-tuple-element.34), channel_id=1, source_target_pairs={{16,0},{32,16},{48,32},{64,48},{80,64},{96,80},{112,96},{17,1},{33... | collective-permute-start | bytes 98312 | tf_op jit(solution)/shard_map/ppermute | solution.py:19
  75.2 8.2 %collective-permute-start.6 = (bf16[64,4,1,64]{0,3,2,1:T(8,128)(2,1)S(1)}, bf16[64,4,1,64]{0,3,2,1:T(8,128)(2,1)S(1)}, u32[]{:S(2)}, u32[]{:S(2)}) collective-permute-start(bf16[64,4,1,64]{0,3,2,1:T(8,128)(2,1)S(1)} %get-tuple-element.24), channel_id=1, source_target_pairs={{0,1},{1,2},{2,3},{3,4},{4,5},{5,6},{6,7},{7,8},{8,9},{9,10},{10,1... | collective-permute-start | bytes 98312 | tf_op jit(solution)/shard_map/ppermute | solution.py:18
  77.5 7.6 %collective-permute-start.7 = (bf16[64,4,1,64]{0,3,2,1:T(8,128)(2,1)S(1)}, bf16[64,4,1,64]{0,3,2,1:T(8,128)(2,1)S(1)}, u32[]{:S(2)}, u32[]{:S(2)}) collective-permute-start(bf16[64,4,1,64]{0,3,2,1:T(8,128)(2,1)S(1)} %get-tuple-element.25), channel_id=1, source_target_pairs={{1,0},{2,1},{3,2},{4,3},{5,4},{6,5},{7,6},{8,7},{9,8},{10,9},{11,1... | collective-permute-start | bytes 98312 | tf_op jit(solution)/shard_map/ppermute | solution.py:19
  89.6 0.9 copy-start.15
  96.6 6.4 %collective-permute-start.8 = (bf16[128,1,4,64]{0,3,2,1:T(8,128)(2,1)S(1)}, bf16[128,1,4,64]{0,3,2,1:T(8,128)(2,1)S(1)}, u32[]{:S(2)}, u32[]{:S(2)}) collective-permute-start(bf16[128,1,4,64]{0,3,2,1:T(8,128)(2,1)S(1)} %get-tuple-element.31), channel_id=1, source_target_pairs={{0,16},{16,32},{32,48},{48,64},{64,80},{80,96},{96,112},{1,17},{17... | collective-permute-start | bytes 196616 | tf_op jit(solution)/shard_map/ppermute | solution.py:18
  100.5 6.5 %collective-permute-start.9 = (bf16[128,1,4,64]{0,3,2,1:T(8,128)(2,1)S(1)}, bf16[128,1,4,64]{0,3,2,1:T(8,128)(2,1)S(1)}, u32[]{:S(2)}, u32[]{:S(2)}) collective-permute-start(bf16[128,1,4,64]{0,3,2,1:T(8,128)(2,1)S(1)} %get-tuple-element.32), channel_id=1, source_target_pairs={{16,0},{32,16},{48,32},{64,48},{80,64},{96,80},{112,96},{17,1},{33... | collective-permute-start | bytes 196616 | tf_op jit(solution)/shard_map/ppermute | solution.py:19
  107.1 7.1 %collective-permute-start.11 = (bf16[128,4,1,64]{0,3,2,1:T(8,128)(2,1)S(1)}, bf16[128,4,1,64]{0,3,2,1:T(8,128)(2,1)S(1)}, u32[]{:S(2)}, u32[]{:S(2)}) collective-permute-start(bf16[128,4,1,64]{0,3,2,1:T(8,128)(2,1)S(1)} %get-tuple-element.23), channel_id=1, source_target_pairs={{1,0},{2,1},{3,2},{4,3},{5,4},{6,5},{7,6},{8,7},{9,8},{10,9},{11,1... | collective-permute-start | bytes 196616 | tf_op jit(solution)/shard_map/ppermute | solution.py:19
  112.0 8.0 %collective-permute-start.10 = (bf16[128,4,1,64]{0,3,2,1:T(8,128)(2,1)S(1)}, bf16[128,4,1,64]{0,3,2,1:T(8,128)(2,1)S(1)}, u32[]{:S(2)}, u32[]{:S(2)}) collective-permute-start(bf16[128,4,1,64]{0,3,2,1:T(8,128)(2,1)S(1)} %get-tuple-element.22), channel_id=1, source_target_pairs={{0,1},{1,2},{2,3},{3,4},{4,5},{5,6},{6,7},{7,8},{8,9},{9,10},{10,1... | collective-permute-start | bytes 196616 | tf_op jit(solution)/shard_map/ppermute | solution.py:18
  114.1 6.5 %copy-start.13 = (bf16[27,128,64]{1,2,0:T(8,128)(2,1)}, bf16[27,128,64]{1,2,0:T(8,128)(2,1)S(1)}, u32[]{:S(2)}) copy-start(bf16[27,128,64]{1,2,0:T(8,128)(2,1)S(1)} %fusion.126) | copy-start | bytes 1327108
  129.2 2.2 copy-start.11
  131.1 1.1 copy-start.5
  131.6 1.5 copy-start.9
  133.4 1.5 copy-start.1
  136.0 1.5 copy-start.3
  139.0 0.8 copy-start.12
  139.0 5.0 %copy-start.7 = (bf16[27,64,32]{1,2,0:T(8,128)(2,1)S(1)}, bf16[27,64,32]{1,2,0:T(8,128)(2,1)}, u32[]{:S(2)}) copy-start(bf16[27,64,32]{1,2,0:T(8,128)(2,1)} %param.5) | copy-start | bytes 331780
  139.8 166.8 %reduce-scatter.2.cloned.1.call-start = ((), (), s32[]{:S(2)}) async-start(), calls=%async_computation.2 | async-start | bytes 1114112 | tf_op jit(solution)/shard_map/reduce_scatter | solution.py:128
  144.3 142.3 %collective-permute-start.13 = (bf16[64,1,8,128]{3,0,2,1:T(8,128)(2,1)S(1)}, bf16[64,1,8,128]{3,0,2,1:T(8,128)(2,1)S(1)}, u32[]{:S(2)}, u32[]{:S(2)}) collective-permute-start(bf16[64,1,8,128]{3,0,2,1:T(8,128)(2,1)S(1)} %get-tuple-element.17), channel_id=1, source_target_pairs={{16,0},{32,16},{48,32},{64,48},{80,64},{96,80},{112,96},{17,1},{33... | collective-permute-start | bytes 393224 | tf_op jit(solution)/shard_map/ppermute | solution.py:19
  145.6 141.0 %collective-permute-start.12 = (bf16[64,1,8,128]{3,0,2,1:T(8,128)(2,1)S(1)}, bf16[64,1,8,128]{3,0,2,1:T(8,128)(2,1)S(1)}, u32[]{:S(2)}, u32[]{:S(2)}) collective-permute-start(bf16[64,1,8,128]{3,0,2,1:T(8,128)(2,1)S(1)} %get-tuple-element.16), channel_id=1, source_target_pairs={{0,16},{16,32},{32,48},{48,64},{64,80},{80,96},{96,112},{1,17},{17... | collective-permute-start | bytes 393224 | tf_op jit(solution)/shard_map/ppermute | solution.py:18
  286.6 8.6 %collective-permute-start.14 = (bf16[64,6,1,128]{3,0,2,1:T(8,128)(2,1)S(1)}, bf16[64,6,1,128]{3,0,2,1:T(8,128)(2,1)S(1)}, u32[]{:S(2)}, u32[]{:S(2)}) collective-permute-start(bf16[64,6,1,128]{3,0,2,1:T(8,128)(2,1)S(1)} %get-tuple-element.14), channel_id=1, source_target_pairs={{0,1},{1,2},{2,3},{3,4},{4,5},{5,6},{6,7},{7,8},{8,9},{9,10},{10,1... | collective-permute-start | bytes 294920 | tf_op jit(solution)/shard_map/ppermute | solution.py:18
  288.5 8.2 %collective-permute-start.15 = (bf16[64,6,1,128]{3,0,2,1:T(8,128)(2,1)S(1)}, bf16[64,6,1,128]{3,0,2,1:T(8,128)(2,1)S(1)}, u32[]{:S(2)}, u32[]{:S(2)}) collective-permute-start(bf16[64,6,1,128]{3,0,2,1:T(8,128)(2,1)S(1)} %get-tuple-element.15), channel_id=1, source_target_pairs={{1,0},{2,1},{3,2},{4,3},{5,4},{6,5},{7,6},{8,7},{9,8},{10,9},{11,1... | collective-permute-start | bytes 294920 | tf_op jit(solution)/shard_map/ppermute | solution.py:19
Sparse Core Ops, SparseCore 0:
  139.9 144.7 all-reduce.5
Sparse Core Ops, SparseCore 1:
  144.6 66.4 reduce-scatter.1
where the time goes:
time: 349 us; the launch traced here: 348 us
  waiting for transfers between devices  154 us (44%)
  blocking collectives  57 us (16%)
  starting transfers between devices  52.8 us (15%)
  matrix products  43.6 us (12%)
  between operations  16.6 us (5%)
  local copies, waits for them, and re-layouts  14.2 us (4%)
  other arithmetic  10.1 us (3%)
    psum x1, waiting for transfers between devices, shards(): grad_three = lax.psum(partial_three, ('depth', 'height')) * scale_three  135 us
    psum x1, blocking collectives, shards(): depth_summed = lax.psum(partial_four.astype(jnp.bfloat16), 'depth')  33.3 us
    ppermute x8, starting transfers between devices, extended_2(): after = lax.ppermute(first, axis, down)  28.1 us
    ppermute x8, starting transfers between devices, extended_2(): before = lax.ppermute(last, axis, up)  24.6 us
    all_gather x1, blocking collectives, shards(): full_bank = lax.all_gather(filters_four, 'height', axis=1, tiled=True)  23.7 us
    dot_general x54, matrix products, forward_taps(): jnp.einsum('oi,idhw->odhw', weights[9 * first + 3 * second + third], wind...  16.9 us
    dot_general x54, matrix products, weight_taps(): jnp.einsum('odhw,idhw->oi', delta, window_piece, preferred_element_type=j...  14.4 us
    dot_general x54, matrix products, transpose_taps(): jnp.einsum('oi,odhw->idhw', weights[9 * first + 3 * second + third], wind...  12.3 us
  transfers between devices with their start and end apart: 18, of which 9 were waited for; matrix products, arithmetic and copies ran while one was open for 5% of the time, Pallas kernels for 0%

commit v1 on v0

--- a/solution.py
+++ b/solution.py
@@ -117,7 +117,9 @@
         channels_mid, half_depth, 2, half_height, 2, half_width, 2
     )
     pooled = (jnp.sum(hidden, axis=(2, 4, 6)) * 0.125).astype(jnp.bfloat16)
-    full_bank = lax.all_gather(filters_four, "height", axis=1, tiled=True)
+    full_bank = jnp.concatenate(
+        lax.all_to_all(jnp.stack([filters_four] * lax.axis_size("height")), "height", 0, 0), axis=1
+    )
     rimmed = extended_2(pooled, (("depth", 1), ("height", 2)), 1)
     pooled_pad = pad_width(rimmed)
     act_four = forward_taps(pooled_pad, full_bank, half_depth, half_height, half_width)

time: 349 us -> 337 us (0.966)
  blocking collectives: 57 us -> 33.3 us
  starting transfers between devices: 52.8 us -> 61.2 us
    all_gather x1 -> x0, blocking collectives: 23.7 us -> none  [shards(): full_bank = lax.all_gather(filters_four, 'height', axis=1, tiled=True)]
    all_to_all x0 -> x1, starting transfers between devices: none -> 8.64 us  [shards(): lax.all_to_all(jnp.stack([filters_four] * lax.axis_size('height')), 'heig...]
  transfers between devices with their start and end apart: 18 -> 19, of which waited for: 9 -> 10; matrix products, arithmetic and copies ran while one was open for 5% -> 6% of each run, Pallas kernels for 0% -> 0%
where the time goes in v1:
time: 337 us; the launch traced here: 336 us
  waiting for transfers between devices  153 us (45%)
  starting transfers between devices  61.2 us (18%)
  matrix products  44 us (13%)
  blocking collectives  33.3 us (10%)
  local copies, waits for them, and re-layouts  17.1 us (5%)
  between operations  16.7 us (5%)
  other arithmetic  10.5 us (3%)
    psum x1, waiting for transfers between devices, shards(): grad_three = lax.psum(partial_three, ('depth', 'height')) * scale_three  135 us
    psum x1, blocking collectives, shards(): depth_summed = lax.psum(partial_four.astype(jnp.bfloat16), 'depth')  33.3 us
    ppermute x8, starting transfers between devices, extended_2(): after = lax.ppermute(first, axis, down)  28.4 us
    ppermute x8, starting transfers between devices, extended_2(): before = lax.ppermute(last, axis, up)  24.1 us
    dot_general x54, matrix products, forward_taps(): jnp.einsum('oi,idhw->odhw', weights[9 * first + 3 * second + third], wind...  17.3 us
    dot_general x54, matrix products, weight_taps(): jnp.einsum('odhw,idhw->oi', delta, window_piece, preferred_element_type=j...  14.5 us
    dot_general x54, matrix products, transpose_taps(): jnp.einsum('oi,odhw->idhw', weights[9 * first + 3 * second + third], wind...  12.3 us
    ppermute x8, waiting for transfers between devices, extended_2(): after = lax.ppermute(first, axis, down)  10.6 us
  transfers between devices with their start and end apart: 19, of which 10 were waited for; matrix products, arithmetic and copies ran while one was open for 6% of the time, Pallas kernels for 0%

profile of v1, /device:TPU:6, one launch (start us, length us, event | category | flops | bytes accessed | tf_op | source)
XLA Modules:
  0.0 336.0 jit_solution(11852271952811573718)
XLA Ops:
  8.0 0.9 fusion.559
  9.0 3.5 %collective-permute-start = (bf16[32,1,8,128]{3,0,2,1:T(8,128)(2,1)S(1)}, bf16[32,1,8,128]{3,0,2,1:T(8,128)(2,1)S(1)}, u32[]{:S(2)}, u32[]{:S(2)}) collective-permute-start(bf16[32,1,8,128]{3,0,2,1:T(8,128)(2,1)S(1)} %copy.455), channel_id=1, source_target_pairs={{0,16},{16,32},{32,48},{48,64},{64,80},{80,96},{96,112},{1,17},{17... | collective-permute-start | bytes 196616 | tf_op jit(solution)/shard_map/ppermute | solution.py:18
  12.5 1.3 collective-permute-start.1
  13.8 0.6 collective-permute-done
  14.4 1.2 constant_dynamic-update-slice_fusion.6
  15.6 3.1 collective-permute-done.1
  18.7 1.9 collective-permute-start.2
  20.6 6.0 %collective-permute-start.3 = (bf16[32,6,1,128]{3,0,2,1:T(8,128)(2,1)S(1)}, bf16[32,6,1,128]{3,0,2,1:T(8,128)(2,1)S(1)}, u32[]{:S(2)}, u32[]{:S(2)}) collective-permute-start(bf16[32,6,1,128]{3,0,2,1:T(8,128)(2,1)S(1)} %get-tuple-element.19), channel_id=1, source_target_pairs={{1,0},{2,1},{3,2},{4,3},{5,4},{6,5},{7,6},{8,7},{9,8},{10,9},{11,1... | collective-permute-start | bytes 147464 | tf_op jit(solution)/shard_map/ppermute | solution.py:19
  27.1 1.4 collective-permute-done.3
  28.4 0.5 fusion.212
  29.2 0.4 fusion.320
  30.0 0.4 fusion.314
  30.7 0.4 fusion.308
  31.1 0.4 convolution_bitcast_fusion.10
  32.2 0.4 convolution_bitcast_fusion.8
  32.9 0.4 convolution_bitcast_fusion.4
  33.6 0.4 convolution_bitcast_fusion.6
  34.7 0.4 convolution_add_fusion.4
  36.9 0.4 fusion.22
  37.2 0.7 fusion.27
  38.3 1.7 add_multiply_fusion
  40.0 2.0 copy.144
  41.9 2.9 reduce_sum.9
  44.9 4.6 %collective-permute-start.4 = (bf16[64,1,4,64]{0,3,2,1:T(8,128)(2,1)S(1)}, bf16[64,1,4,64]{0,3,2,1:T(8,128)(2,1)S(1)}, u32[]{:S(2)}, u32[]{:S(2)}) collective-permute-start(bf16[64,1,4,64]{0,3,2,1:T(8,128)(2,1)S(1)} %get-tuple-element.33), channel_id=1, source_target_pairs={{0,16},{16,32},{32,48},{48,64},{64,80},{80,96},{96,112},{1,17},{17... | collective-permute-start | bytes 98312 | tf_op jit(solution)/shard_map/ppermute | solution.py:18
  49.5 1.3 collective-permute-start.5
  51.0 1.3 reshape.215
  52.3 8.6 %all-to-all-start = ((bf16[16,2,6912]{2,1,0:T(2,128)(2,1)}), bf16[16,2,6912]{2,1,0:T(2,128)(2,1)S(1)}, u32[]{:S(2)}, u32[]{:S(2)}) async-start(bf16[16,2,6912]{2,1,0:T(2,128)(2,1)} %reshape.215), calls=%async_computation | async-start | bytes 884736 | tf_op jit(solution)/shard_map/all_to_all | solution.py:121
  61.0 2.1 collective-permute-start.6
  63.1 5.9 %collective-permute-start.7 = (bf16[64,4,1,64]{0,3,2,1:T(8,128)(2,1)S(1)}, bf16[64,4,1,64]{0,3,2,1:T(8,128)(2,1)S(1)}, u32[]{:S(2)}, u32[]{:S(2)}) collective-permute-start(bf16[64,4,1,64]{0,3,2,1:T(8,128)(2,1)S(1)} %get-tuple-element.25), channel_id=1, source_target_pairs={{1,0},{2,1},{3,2},{4,3},{5,4},{6,5},{7,6},{8,7},{9,8},{10,9},{11,1... | collective-permute-start | bytes 98312 | tf_op jit(solution)/shard_map/ppermute | solution.py:19
  69.0 1.8 collective-permute-done.6
  71.1 0.9 pad_maximum_fusion.7
  72.0 0.5 reshape.216
  78.0 1.1 fusion.283
  84.8 3.7 %collective-permute-start.8 = (bf16[128,1,4,64]{0,3,2,1:T(8,128)(2,1)S(1)}, bf16[128,1,4,64]{0,3,2,1:T(8,128)(2,1)S(1)}, u32[]{:S(2)}, u32[]{:S(2)}) collective-permute-start(bf16[128,1,4,64]{0,3,2,1:T(8,128)(2,1)S(1)} %get-tuple-element.31), channel_id=1, source_target_pairs={{0,16},{16,32},{32,48},{48,64},{64,80},{80,96},{96,112},{1,17},{17... | collective-permute-start | bytes 196616 | tf_op jit(solution)/shard_map/ppermute | solution.py:18
  88.4 1.3 collective-permute-start.9
  89.9 0.4 collective-permute-done.8
  90.3 4.5 %collective-permute-done.9 = bf16[128,1,4,64]{0,3,2,1:T(8,128)(2,1)S(1)} collective-permute-done((bf16[128,1,4,64]{0,3,2,1:T(8,128)(2,1)S(1)}, bf16[128,1,4,64]{0,3,2,1:T(8,128)(2,1)S(1)}, u32[]{:S(2)}, u32[]{:S(2)}) %collective-permute-start.9) | collective-permute-done | bytes 65568 | tf_op jit(solution)/shard_map/ppermute | solution.py:19
  94.9 5.0 %collective-permute-start.11 = (bf16[128,4,1,64]{0,3,2,1:T(8,128)(2,1)S(1)}, bf16[128,4,1,64]{0,3,2,1:T(8,128)(2,1)S(1)}, u32[]{:S(2)}, u32[]{:S(2)}) collective-permute-start(bf16[128,4,1,64]{0,3,2,1:T(8,128)(2,1)S(1)} %get-tuple-element.23), channel_id=1, source_target_pairs={{1,0},{2,1},{3,2},{4,3},{5,4},{6,5},{7,6},{8,7},{9,8},{10,9},{11,1... | collective-permute-start | bytes 196616 | tf_op jit(solution)/shard_map/ppermute | solution.py:19
  99.9 1.9 collective-permute-start.10
  102.1 0.8 copy-done.14
  102.8 5.1 %collective-permute-done.10 = bf16[128,4,1,64]{0,3,2,1:T(8,128)(2,1)S(1)} collective-permute-done((bf16[128,4,1,64]{0,3,2,1:T(8,128)(2,1)S(1)}, bf16[128,4,1,64]{0,3,2,1:T(8,128)(2,1)S(1)}, u32[]{:S(2)}, u32[]{:S(2)}) %collective-permute-start.10) | collective-permute-done | bytes 65568 | tf_op jit(solution)/shard_map/ppermute | solution.py:18
  113.0 0.4 broadcast_in_dim.10
  113.3 1.5 broadcast_in_dim.11
  114.8 2.2 copy.200
  117.0 1.9 fusion.210
  126.9 0.7 copy-done.13
  127.7 0.8 fusion.124
  128.5 3.4 copy.229
  132.1 1.3 collective-permute-start.13
  133.4 4.6 %collective-permute-start.12 = (bf16[64,1,8,128]{3,0,2,1:T(8,128)(2,1)S(1)}, bf16[64,1,8,128]{3,0,2,1:T(8,128)(2,1)S(1)}, u32[]{:S(2)}, u32[]{:S(2)}) collective-permute-start(bf16[64,1,8,128]{3,0,2,1:T(8,128)(2,1)S(1)} %get-tuple-element.16), channel_id=1, source_target_pairs={{0,16},{16,32},{32,48},{48,64},{64,80},{80,96},{96,112},{1,17},{17... | collective-permute-start | bytes 393224 | tf_op jit(solution)/shard_map/ppermute | solution.py:18
  138.0 134.7 %all-reduce.6.cloned.1.call-done = f32[27,64,32]{1,2,0:T(8,128)} async-done(((f32[27,64,32]{1,2,0:T(8,128)}), f32[27,64,32]{1,2,0:T(8,128)}) %all-reduce.6.cloned.1.call-update) | async-done | bytes 221200 | tf_op jit(solution)/shard_map/psum | solution.py:144
  272.7 1.8 broadcast_multiply_fusion
  274.5 1.9 collective-permute-start.14
  276.5 6.3 %collective-permute-start.15 = (bf16[64,6,1,128]{3,0,2,1:T(8,128)(2,1)S(1)}, bf16[64,6,1,128]{3,0,2,1:T(8,128)(2,1)S(1)}, u32[]{:S(2)}, u32[]{:S(2)}) collective-permute-start(bf16[64,6,1,128]{3,0,2,1:T(8,128)(2,1)S(1)} %get-tuple-element.15), channel_id=1, source_target_pairs={{1,0},{2,1},{3,2},{4,3},{5,4},{6,5},{7,6},{8,7},{9,8},{10,9},{11,1... | collective-permute-start | bytes 294920 | tf_op jit(solution)/shard_map/ppermute | solution.py:19
  283.2 1.5 collective-permute-done.15
  285.3 1.8 select_maximum_fusion
  288.3 0.4 fusion.242
  290.9 0.4 convolution_bitcast_fusion.15
  291.4 0.4 convolution_bitcast_fusion.18
  292.4 0.7 fusion.52
  293.3 0.5 fusion.53
  293.7 0.8 copy.230
  294.6 33.3 %psum.16 = bf16[27,8,64]{2,0,1:T(8,128)(2,1)S(1)} all-reduce(bf16[27,8,64]{2,0,1:T(8,128)(2,1)} %reduce-scatter.2.cloned.1.call-done), channel_id=1, replica_groups=mesh['depth'=8,'height'=16] {'depth'}, use_global_device_ids=true, to_apply=%region_2.3 | all-reduce | flops 13824 | bytes 55296 | tf_op jit(solution)/shard_map/psum | solution.py:128
  327.9 0.7 copy.231
  (213 shorter events, 35.7 us)
Async XLA Ops:
  8.0 18.7 %copy-start = (bf16[32,4,8,128]{3,2,1,0:T(8,128)(2,1)S(1)}, bf16[32,4,8,128]{3,2,1,0:T(8,128)(2,1)}, u32[]{:S(2)}) copy-start(bf16[32,4,8,128]{3,2,1,0:T(8,128)(2,1)} %param.4) | copy-start | bytes 786436
  8.0 18.7 %copy-start.7 = (bf16[27,64,32]{1,2,0:T(8,128)(2,1)S(1)}, bf16[27,64,32]{1,2,0:T(8,128)(2,1)}, u32[]{:S(2)}) copy-start(bf16[27,64,32]{1,2,0:T(8,128)(2,1)} %param.5) | copy-start | bytes 331780
  9.0 5.4 %collective-permute-start = (bf16[32,1,8,128]{3,0,2,1:T(8,128)(2,1)S(1)}, bf16[32,1,8,128]{3,0,2,1:T(8,128)(2,1)S(1)}, u32[]{:S(2)}, u32[]{:S(2)}) collective-permute-start(bf16[32,1,8,128]{3,0,2,1:T(8,128)(2,1)S(1)} %copy.455), channel_id=1, source_target_pairs={{0,16},{16,32},{32,48},{48,64},{64,80},{80,96},{96,112},{1,17},{17... | collective-permute-start | bytes 196616 | tf_op jit(solution)/shard_map/ppermute | solution.py:18
  12.5 6.2 %collective-permute-start.1 = (bf16[32,1,8,128]{3,0,2,1:T(8,128)(2,1)S(1)}, bf16[32,1,8,128]{3,0,2,1:T(8,128)(2,1)S(1)}, u32[]{:S(2)}, u32[]{:S(2)}) collective-permute-start(bf16[32,1,8,128]{3,0,2,1:T(8,128)(2,1)S(1)} %copy.456), channel_id=1, source_target_pairs={{16,0},{32,16},{48,32},{64,48},{80,64},{96,80},{112,96},{17,1},{33... | collective-permute-start | bytes 196616 | tf_op jit(solution)/shard_map/ppermute | solution.py:19
  15.5 19.9 %copy-start.4 = (bf16[32,5,8,128]{3,0,2,1:T(8,128)(2,1)}, bf16[32,5,8,128]{3,0,2,1:T(8,128)(2,1)S(1)}, u32[]{:S(2)}) copy-start(bf16[32,5,8,128]{3,0,2,1:T(8,128)(2,1)S(1)} %get-tuple-element.28) | copy-start | bytes 983044
  18.7 19.6 %copy-start.2 = (bf16[32,5,8,128]{3,0,2,1:T(8,128)(2,1)}, bf16[32,5,8,128]{3,0,2,1:T(8,128)(2,1)S(1)}, u32[]{:S(2)}) copy-start(bf16[32,5,8,128]{3,0,2,1:T(8,128)(2,1)S(1)} %get-tuple-element.35) | copy-start | bytes 983044
  18.7 8.3 %collective-permute-start.2 = (bf16[32,6,1,128]{3,0,2,1:T(8,128)(2,1)S(1)}, bf16[32,6,1,128]{3,0,2,1:T(8,128)(2,1)S(1)}, u32[]{:S(2)}, u32[]{:S(2)}) collective-permute-start(bf16[32,6,1,128]{3,0,2,1:T(8,128)(2,1)S(1)} %get-tuple-element.18), channel_id=1, source_target_pairs={{0,1},{1,2},{2,3},{3,4},{4,5},{5,6},{6,7},{7,8},{8,9},{9,10},{10,1... | collective-permute-start | bytes 147464 | tf_op jit(solution)/shard_map/ppermute | solution.py:18
  20.6 7.8 %collective-permute-start.3 = (bf16[32,6,1,128]{3,0,2,1:T(8,128)(2,1)S(1)}, bf16[32,6,1,128]{3,0,2,1:T(8,128)(2,1)S(1)}, u32[]{:S(2)}, u32[]{:S(2)}) collective-permute-start(bf16[32,6,1,128]{3,0,2,1:T(8,128)(2,1)S(1)} %get-tuple-element.19), channel_id=1, source_target_pairs={{1,0},{2,1},{3,2},{4,3},{5,4},{6,5},{7,6},{8,7},{9,8},{10,9},{11,1... | collective-permute-start | bytes 147464 | tf_op jit(solution)/shard_map/ppermute | solution.py:19
  27.0 9.8 %copy-start.11 = (bf16[32,6,1,128]{3,0,2,1:T(8,128)(2,1)}, bf16[32,6,1,128]{3,0,2,1:T(8,128)(2,1)S(1)}, u32[]{:S(2)}) copy-start(bf16[32,6,1,128]{3,0,2,1:T(8,128)(2,1)S(1)} %collective-permute-done.2) | copy-start | bytes 147460
  28.4 9.5 %copy-start.9 = (bf16[32,6,1,128]{3,0,2,1:T(8,128)(2,1)}, bf16[32,6,1,128]{3,0,2,1:T(8,128)(2,1)S(1)}, u32[]{:S(2)}) copy-start(bf16[32,6,1,128]{3,0,2,1:T(8,128)(2,1)S(1)} %collective-permute-done.3) | copy-start | bytes 147460
  41.9 8.9 %copy-start.17 = (bf16[27,8,64]{2,1,0:T(8,128)(2,1)S(1)}, bf16[27,8,64]{2,1,0:T(8,128)(2,1)}, u32[]{:S(2)}) copy-start(bf16[27,8,64]{2,1,0:T(8,128)(2,1)} %param.6) | copy-start | bytes 82948
  44.9 16.0 %collective-permute-start.4 = (bf16[64,1,4,64]{0,3,2,1:T(8,128)(2,1)S(1)}, bf16[64,1,4,64]{0,3,2,1:T(8,128)(2,1)S(1)}, u32[]{:S(2)}, u32[]{:S(2)}) collective-permute-start(bf16[64,1,4,64]{0,3,2,1:T(8,128)(2,1)S(1)} %get-tuple-element.33), channel_id=1, source_target_pairs={{0,16},{16,32},{32,48},{48,64},{64,80},{80,96},{96,112},{1,17},{17... | collective-permute-start | bytes 98312 | tf_op jit(solution)/shard_map/ppermute | solution.py:18
  49.5 11.4 %collective-permute-start.5 = (bf16[64,1,4,64]{0,3,2,1:T(8,128)(2,1)S(1)}, bf16[64,1,4,64]{0,3,2,1:T(8,128)(2,1)S(1)}, u32[]{:S(2)}, u32[]{:S(2)}) collective-permute-start(bf16[64,1,4,64]{0,3,2,1:T(8,128)(2,1)S(1)} %get-tuple-element.34), channel_id=1, source_target_pairs={{16,0},{32,16},{48,32},{64,48},{80,64},{96,80},{112,96},{17,1},{33... | collective-permute-start | bytes 98312 | tf_op jit(solution)/shard_map/ppermute | solution.py:19
  52.3 19.7 %all-to-all-start = ((bf16[16,2,6912]{2,1,0:T(2,128)(2,1)}), bf16[16,2,6912]{2,1,0:T(2,128)(2,1)S(1)}, u32[]{:S(2)}, u32[]{:S(2)}) async-start(bf16[16,2,6912]{2,1,0:T(2,128)(2,1)} %reshape.215), calls=%async_computation | async-start | bytes 884736 | tf_op jit(solution)/shard_map/all_to_all | solution.py:121
  60.9 211.8 %all-reduce.6.cloned.1.call-start = ((), (), s32[]{:S(2)}) async-start(), calls=%async_computation.2 | async-start | bytes 884736 | tf_op jit(solution)/shard_map/psum | solution.py:144
  61.0 9.8 %collective-permute-start.6 = (bf16[64,4,1,64]{0,3,2,1:T(8,128)(2,1)S(1)}, bf16[64,4,1,64]{0,3,2,1:T(8,128)(2,1)S(1)}, u32[]{:S(2)}, u32[]{:S(2)}) collective-permute-start(bf16[64,4,1,64]{0,3,2,1:T(8,128)(2,1)S(1)} %get-tuple-element.24), channel_id=1, source_target_pairs={{0,1},{1,2},{2,3},{3,4},{4,5},{5,6},{6,7},{7,8},{8,9},{9,10},{10,1... | collective-permute-start | bytes 98312 | tf_op jit(solution)/shard_map/ppermute | solution.py:18
  63.1 7.8 %collective-permute-start.7 = (bf16[64,4,1,64]{0,3,2,1:T(8,128)(2,1)S(1)}, bf16[64,4,1,64]{0,3,2,1:T(8,128)(2,1)S(1)}, u32[]{:S(2)}, u32[]{:S(2)}) collective-permute-start(bf16[64,4,1,64]{0,3,2,1:T(8,128)(2,1)S(1)} %get-tuple-element.25), channel_id=1, source_target_pairs={{1,0},{2,1},{3,2},{4,3},{5,4},{6,5},{7,6},{8,7},{9,8},{10,9},{11,1... | collective-permute-start | bytes 98312 | tf_op jit(solution)/shard_map/ppermute | solution.py:19
  70.9 6.4 %copy-start.6 = (bf16[64,4,1,64]{0,3,2,1:T(8,128)(2,1)}, bf16[64,4,1,64]{0,3,2,1:T(8,128)(2,1)S(1)}, u32[]{:S(2)}) copy-start(bf16[64,4,1,64]{0,3,2,1:T(8,128)(2,1)S(1)} %collective-permute-done.7) | copy-start | bytes 98308
  77.1 0.9 copy-start.18
  77.6 2.0 copy-start.16
  79.1 1.8 copy-start.15
  84.8 5.6 %collective-permute-start.8 = (bf16[128,1,4,64]{0,3,2,1:T(8,128)(2,1)S(1)}, bf16[128,1,4,64]{0,3,2,1:T(8,128)(2,1)S(1)}, u32[]{:S(2)}, u32[]{:S(2)}) collective-permute-start(bf16[128,1,4,64]{0,3,2,1:T(8,128)(2,1)S(1)} %get-tuple-element.31), channel_id=1, source_target_pairs={{0,16},{16,32},{32,48},{48,64},{64,80},{80,96},{96,112},{1,17},{17... | collective-permute-start | bytes 196616 | tf_op jit(solution)/shard_map/ppermute | solution.py:18
  88.4 6.4 %collective-permute-start.9 = (bf16[128,1,4,64]{0,3,2,1:T(8,128)(2,1)S(1)}, bf16[128,1,4,64]{0,3,2,1:T(8,128)(2,1)S(1)}, u32[]{:S(2)}, u32[]{:S(2)}) collective-permute-start(bf16[128,1,4,64]{0,3,2,1:T(8,128)(2,1)S(1)} %get-tuple-element.32), channel_id=1, source_target_pairs={{16,0},{32,16},{48,32},{64,48},{80,64},{96,80},{112,96},{17,1},{33... | collective-permute-start | bytes 196616 | tf_op jit(solution)/shard_map/ppermute | solution.py:19
  94.9 7.2 %collective-permute-start.11 = (bf16[128,4,1,64]{0,3,2,1:T(8,128)(2,1)S(1)}, bf16[128,4,1,64]{0,3,2,1:T(8,128)(2,1)S(1)}, u32[]{:S(2)}, u32[]{:S(2)}) collective-permute-start(bf16[128,4,1,64]{0,3,2,1:T(8,128)(2,1)S(1)} %get-tuple-element.23), channel_id=1, source_target_pairs={{1,0},{2,1},{3,2},{4,3},{5,4},{6,5},{7,6},{8,7},{9,8},{10,9},{11,1... | collective-permute-start | bytes 196616 | tf_op jit(solution)/shard_map/ppermute | solution.py:19
  99.9 8.0 %collective-permute-start.10 = (bf16[128,4,1,64]{0,3,2,1:T(8,128)(2,1)S(1)}, bf16[128,4,1,64]{0,3,2,1:T(8,128)(2,1)S(1)}, u32[]{:S(2)}, u32[]{:S(2)}) collective-permute-start(bf16[128,4,1,64]{0,3,2,1:T(8,128)(2,1)S(1)} %get-tuple-element.22), channel_id=1, source_target_pairs={{0,1},{1,2},{2,3},{3,4},{4,5},{5,6},{6,7},{7,8},{8,9},{9,10},{10,1... | collective-permute-start | bytes 196616 | tf_op jit(solution)/shard_map/ppermute | solution.py:18
  102.0 0.8 copy-start.14
  117.0 2.2 copy-start.12
  119.0 1.1 copy-start.5
  119.5 1.5 copy-start.10
  121.2 1.5 copy-start.1
  123.9 1.5 copy-start.3
  126.8 0.8 copy-start.13
  126.8 5.1 %copy-start.8 = (bf16[27,64,32]{1,2,0:T(8,128)(2,1)S(1)}, bf16[27,64,32]{1,2,0:T(8,128)(2,1)}, u32[]{:S(2)}) copy-start(bf16[27,64,32]{1,2,0:T(8,128)(2,1)} %param.5) | copy-start | bytes 331780
  127.6 166.9 %reduce-scatter.2.cloned.1.call-start = ((), (), s32[]{:S(2)}) async-start(), calls=%async_computation.3 | async-start | bytes 1114112 | tf_op jit(solution)/shard_map/reduce_scatter | solution.py:130
  132.1 142.4 %collective-permute-start.13 = (bf16[64,1,8,128]{3,0,2,1:T(8,128)(2,1)S(1)}, bf16[64,1,8,128]{3,0,2,1:T(8,128)(2,1)S(1)}, u32[]{:S(2)}, u32[]{:S(2)}) collective-permute-start(bf16[64,1,8,128]{3,0,2,1:T(8,128)(2,1)S(1)} %get-tuple-element.17), channel_id=1, source_target_pairs={{16,0},{32,16},{48,32},{64,48},{80,64},{96,80},{112,96},{17,1},{33... | collective-permute-start | bytes 393224 | tf_op jit(solution)/shard_map/ppermute | solution.py:19
  133.4 141.1 %collective-permute-start.12 = (bf16[64,1,8,128]{3,0,2,1:T(8,128)(2,1)S(1)}, bf16[64,1,8,128]{3,0,2,1:T(8,128)(2,1)S(1)}, u32[]{:S(2)}, u32[]{:S(2)}) collective-permute-start(bf16[64,1,8,128]{3,0,2,1:T(8,128)(2,1)S(1)} %get-tuple-element.16), channel_id=1, source_target_pairs={{0,16},{16,32},{32,48},{48,64},{64,80},{80,96},{96,112},{1,17},{17... | collective-permute-start | bytes 393224 | tf_op jit(solution)/shard_map/ppermute | solution.py:18
  274.5 8.6 %collective-permute-start.14 = (bf16[64,6,1,128]{3,0,2,1:T(8,128)(2,1)S(1)}, bf16[64,6,1,128]{3,0,2,1:T(8,128)(2,1)S(1)}, u32[]{:S(2)}, u32[]{:S(2)}) collective-permute-start(bf16[64,6,1,128]{3,0,2,1:T(8,128)(2,1)S(1)} %get-tuple-element.14), channel_id=1, source_target_pairs={{0,1},{1,2},{2,3},{3,4},{4,5},{5,6},{6,7},{7,8},{8,9},{9,10},{10,1... | collective-permute-start | bytes 294920 | tf_op jit(solution)/shard_map/ppermute | solution.py:18
  276.5 8.2 %collective-permute-start.15 = (bf16[64,6,1,128]{3,0,2,1:T(8,128)(2,1)S(1)}, bf16[64,6,1,128]{3,0,2,1:T(8,128)(2,1)S(1)}, u32[]{:S(2)}, u32[]{:S(2)}) collective-permute-start(bf16[64,6,1,128]{3,0,2,1:T(8,128)(2,1)S(1)} %get-tuple-element.15), channel_id=1, source_target_pairs={{1,0},{2,1},{3,2},{4,3},{5,4},{6,5},{7,6},{8,7},{9,8},{10,9},{11,1... | collective-permute-start | bytes 294920 | tf_op jit(solution)/shard_map/ppermute | solution.py:19
Sparse Core Ops, SparseCore 0:
  127.8 144.8 all-reduce.5
Sparse Core Ops, SparseCore 1:
  132.4 66.5 reduce-scatter.1
